TPU v7x, 512 devices: a whole 4x8x8 slice. The times are simulated.
512 devices in a mesh: section: 32 (over y, z_hi), dp: 16 (over z_lo, x, core).
Axes of the slice: x: 4, y: 8, z: 8 (z_hi: 4, z_lo: 2; z = z_hi * 2 + z_lo), core: 2. Of those that a mesh axis runs over, the one named last changes fastest.
Arguments:
- block_inputs: bfloat16 [32, 4096, 2048], P('section', 'dp'), may hold values from -6 to 6
- target: bfloat16 [4096, 2048], P('dp'), may hold values from -6 to 6
- frozen_weight: bfloat16 [32, 2048, 2048], P('section', 'dp'), may hold values from -0.125 to 0.125
- adapter_down_weight: bfloat16 [32, 2048, 128], P('section', 'dp'), may hold values from -0.125 to 0.125
- adapter_up_weight: bfloat16 [32, 2048, 128], P('section', 'dp'), may hold values from -0.5 to 0.5
- start_modulation: bfloat16 [32, 16, 6144], P('section'), may hold values from -1.1953125 to 1.1953125
- finish_modulation: bfloat16 [32, 16, 6144], P('section'), may hold values from -1.1953125 to 1.1953125
- level_pairs: int32 [128, 2], P('dp'), may hold values from 0 to 15
Outputs:
- input_grads: bfloat16 [32, 4096, 2048], P('section', 'dp')
- down_grad: float32 [32, 2048, 128], P('section', 'dp')
- up_grad: float32 [32, 2048, 128], P('section', 'dp')
Inputs may be any that keep to these rules, and one draw needn't show every extreme that they name: `level_pairs`: each row holds the start and the end time level of one micro-batch.
All inputs are finite; a program needn't handle non-finite values.
Results may differ from a plain program's by a relative error of at most 0.038.
Values may be sent and summed in bfloat16 or wider, within the bound.
No kernel may reach another device: no remote copies, remote signals or barrier semaphores. Data moves between devices by JAX's collectives and lax.ppermute only.
A program may use at most 64 MiB of HBM per device.

v0:
```python
import math

import jax
import jax.numpy as jnp
from jax import lax
from jax.sharding import PartitionSpec as P

epsilon_norm = 1e-06
contract_rows = (((0,), (0,)), ((), ()))


def shifted(value, axis, steps):
    count = lax.axis_size(axis)
    first, last = (max(0, -steps), min(count, count - steps))
    return lax.ppermute(value, axis, [(source, source + steps) for source in range(first, last)])


def activation(values):
    return jax.nn.gelu(values, approximate=True)


def row_modulation(from_table, to_table, level_pairs, block_rows):
    levels = from_table.shape[0]
    ladder = jnp.arange(levels, dtype=jnp.int32)[None, :]
    hot_from = (level_pairs[:, 0:1] == ladder).astype(jnp.bfloat16)
    hot_to = (level_pairs[:, 1:2] == ladder).astype(jnp.bfloat16)
    per_batch = jnp.dot(hot_from, from_table, preferred_element_type=jnp.float32) + jnp.dot(
        hot_to, to_table, preferred_element_type=jnp.float32
    )
    return jnp.repeat(per_batch, block_rows, axis=0)


def forward_sweep(inputs, modulation, weight, down_projected, up_projected):
    model_width = inputs.shape[1]
    shift_vec = modulation[:, :model_width]
    scale_vec = modulation[:, model_width : 2 * model_width]
    values = inputs.astype(jnp.float32)
    inverse_rms = lax.rsqrt(jnp.mean(values * values, axis=1, keepdims=True) + epsilon_norm)
    normed = values * inverse_rms
    modulated = (normed * (1.0 + scale_vec) + shift_vec).astype(jnp.bfloat16)
    lowrank = jnp.dot(modulated, down_projected, preferred_element_type=jnp.float32).astype(
        jnp.bfloat16
    )
    preact = jnp.dot(modulated, weight, preferred_element_type=jnp.float32) + lax.dot_general(
        lowrank, up_projected, (((1,), (1,)), ((), ())), preferred_element_type=jnp.float32
    )
    return (normed, inverse_rms, modulated, lowrank, preact)


def backward_pass(
    cotangent,
    normed,
    inverse_rms,
    preact,
    scale_vec,
    gate_vec,
    weight,
    down_projected,
    up_projected,
):
    upstream = cotangent.astype(jnp.float32)
    outputs_unused, pullback = jax.vjp(activation, preact)
    grad_pre = pullback(upstream * gate_vec)[0].astype(jnp.bfloat16)
    grad_low = jnp.dot(grad_pre, up_projected, preferred_element_type=jnp.float32).astype(
        jnp.bfloat16
    )
    grad_mod = lax.dot_general(
        grad_pre, weight, (((1,), (1,)), ((), ())), preferred_element_type=jnp.float32
    )
    grad_mod = grad_mod + lax.dot_general(
        grad_low, down_projected, (((1,), (1,)), ((), ())), preferred_element_type=jnp.float32
    )
    grad_norm = grad_mod * (1.0 + scale_vec)
    centred = jnp.mean(grad_norm * normed, axis=1, keepdims=True)
    grad_input = upstream + inverse_rms * (grad_norm - normed * centred)
    return (grad_input.astype(jnp.bfloat16), grad_pre, grad_low)


def receive(sent):
    return shifted(sent, "section", -1)


def per_device(
    block_inputs,
    target,
    frozen_weight,
    adapter_down_weight,
    adapter_up_weight,
    start_modulation,
    finish_modulation,
    level_pairs,
):
    block_total = lax.axis_size("section")
    group_total = lax.axis_size("dp")
    section_index = lax.axis_index("section")
    batch_count = level_pairs.shape[0]
    row_count = block_inputs.shape[1]
    block_rows = row_count // batch_count
    model_width = block_inputs.shape[2]
    grad_scale = 1.0 / math.sqrt(row_count * group_total)
    weight = lax.all_gather(frozen_weight[0], "dp", axis=0, tiled=True)
    down_projected, up_projected = (
        lax.all_gather(adapter_down_weight[0], "dp", axis=0, tiled=True),
        lax.all_gather(adapter_up_weight[0], "dp", axis=0, tiled=True),
    )
    rank_count = down_projected.shape[1]
    modulation = row_modulation(start_modulation[0], finish_modulation[0], level_pairs, block_rows)
    scale_vec = modulation[:, model_width : 2 * model_width]
    gate_vec = modulation[:, 2 * model_width :]
    normed, inverse_rms, modulated, lowrank, preact = forward_sweep(
        block_inputs[0], modulation, weight, down_projected, up_projected
    )
    seed_grad = (
        block_inputs[0].astype(jnp.float32)
        + gate_vec * activation(preact)
        - target.astype(jnp.float32)
    ).astype(jnp.bfloat16)
    is_last = section_index == block_total - 1
    turn_count = batch_count + block_total - 1
    empty_send = jnp.zeros((block_rows, model_width), jnp.bfloat16)
    empty_grads = jnp.zeros((row_count, model_width), jnp.bfloat16)

    def rows_of(array, row_start):
        return lax.dynamic_slice_in_dim(array, row_start, block_rows, 0)

    def store(buffer, value, active, row_start):
        kept = jnp.where(active, value, rows_of(buffer, row_start))
        return lax.dynamic_update_slice_in_dim(buffer, kept, row_start, 0)

    def locate(turn_index):
        block_raw = turn_index - (block_total - 1 - section_index)
        active = jnp.logical_and(block_raw >= 0, block_raw < batch_count)
        row_start = jnp.clip(block_raw, 0, batch_count - 1) * block_rows
        return (active, row_start)

    def backward_block(cotangent, row_start):
        return backward_pass(
            cotangent,
            rows_of(normed, row_start),
            rows_of(inverse_rms, row_start),
            rows_of(preact, row_start),
            rows_of(scale_vec, row_start),
            rows_of(gate_vec, row_start),
            weight,
            down_projected,
            up_projected,
        )

    def upstream_for(incoming, row_start):
        return jnp.where(is_last, rows_of(seed_grad, row_start), incoming)

    def work_block(cotangent, row_start):
        grad_input, grad_pre, grad_low = backward_block(cotangent, row_start)
        down_part = lax.dot_general(
            rows_of(modulated, row_start),
            grad_low,
            contract_rows,
            preferred_element_type=jnp.float32,
        )
        up_part = lax.dot_general(
            grad_pre, rows_of(lowrank, row_start), contract_rows, preferred_element_type=jnp.float32
        )
        return (grad_input, down_part, up_part)

    def skip_block(cotangent, row_start):
        empty_part = jnp.zeros((model_width, rank_count), jnp.float32)
        return (cotangent, empty_part, empty_part)

    def turn_accumulate(turn_index, loop_state):
        sent, grads, down_sum, up_sum = loop_state
        incoming = receive(sent)
        active, row_start = locate(turn_index)
        cotangent = upstream_for(incoming, row_start)
        grad_input, down_part, up_part = lax.cond(
            active, work_block, skip_block, cotangent, row_start
        )
        grads = store(grads, grad_input, active, row_start)
        return (grad_input, grads, down_sum + down_part, up_sum + up_part)

    empty_total = jnp.zeros((model_width, rank_count), jnp.float32)
    final_state = lax.fori_loop(
        0, turn_count, turn_accumulate, (empty_send, empty_grads, empty_total, empty_total)
    )
    grads = final_state[1]
    down_total = final_state[2]
    up_total = final_state[3]
    down_grad, up_grad = (
        lax.psum_scatter(
            down_total.astype(jnp.bfloat16), "dp", scatter_dimension=0, tiled=True
        ).astype(jnp.float32),
        lax.psum_scatter(
            up_total.astype(jnp.bfloat16), "dp", scatter_dimension=0, tiled=True
        ).astype(jnp.float32),
    )
    return (grads[None], (down_grad * grad_scale)[None], (up_grad * grad_scale)[None])


def solution(mesh):
    return jax.shard_map(
        per_device,
        mesh=mesh,
        in_specs=(
            P("section", "dp", None),
            P("dp", None),
            P("section", "dp", None),
            P("section", "dp", None),
            P("section", "dp", None),
            P("section", None, None),
            P("section", None, None),
            P("dp", None),
        ),
        out_specs=(P("section", "dp", None), P("section", "dp", None), P("section", "dp", None)),
        check_vma=False,
    )
```

profile of v0, /device:TPU:1, one launch (start us, length us, event | category | flops | bytes accessed | tf_op | source)
XLA Modules:
  0.0 1248.3 jit_solution(843236118145265018)
XLA Ops:
  10.8 25.8 %all-gather.1 = bf16[1,2048,128]{2,1,0:T(8,128)(2,1)} all-gather(bf16[1,128,128]{2,1,0:T(8,128)(2,1)S(1)} %copy-done.7), channel_id=3, replica_groups=mesh['section'=32,'dp'=16] {'dp'}, dimensions={1}, use_global_device_ids=true | all-gather | bytes 557056 | tf_op jit(solution)/shard_map/all_gather | solution.py:103
  36.6 23.7 %all-gather.2 = bf16[1,2048,128]{2,1,0:T(8,128)(2,1)} all-gather(bf16[1,128,128]{2,1,0:T(8,128)(2,1)S(1)} %copy-done.8), channel_id=4, replica_groups=mesh['section'=32,'dp'=16] {'dp'}, dimensions={1}, use_global_device_ids=true | all-gather | bytes 557056 | tf_op jit(solution)/shard_map/all_gather | solution.py:104
  66.4 9.4 all-gather.5.cloned.1.call-done
  75.8 6.2 fusion.35
  87.8 1007.5 %while.22 = (s32[]{:T(128)}, bf16[32,2048]{1,0:T(8,128)(2,1)S(1)}, bf16[256,2048]{1,0:T(8,128)(2,1)}, f32[2048,128]{1,0:T(8,128)S(1)}, f32[2048,128]{1,0:T(8,128...) while((s32[]{:T(128)}, bf16[32,2048]{1,0:T(8,128)(2,1)S(1)}, ...), condition=%wide.region_5.6_spmd.clone, body=%wide.region_1.5_spmd.clone.sunk | while | flops 338890752 | bytes 22578608 | solution.py:181
  89.1 10.0 collective-permute-done
  104.8 8.4 collective-permute-done
  120.2 7.9 collective-permute-done
  135.0 6.2 collective-permute-done
  148.2 10.7 collective-permute-done
  165.8 10.0 collective-permute-done
  182.8 6.3 collective-permute-done
  208.4 8.4 collective-permute-done
  236.0 7.1 collective-permute-done
  250.1 11.1 collective-permute-done
  268.2 8.6 collective-permute-done
  296.1 6.6 collective-permute-done
  309.7 7.4 collective-permute-done
  336.7 7.4 collective-permute-done
  351.1 8.9 collective-permute-done
  367.0 14.7 %collective-permute-done = bf16[32,2048]{1,0:T(8,128)(2,1)S(1)} collective-permute-done((bf16[32,2048]{1,0:T(8,128)(2,1)S(1)}, bf16[32,2048]{1,0:T(8,128)(2,1)S(1)}, u32[]{:S(2)}, u32[]{:S(2)}) %collective-permute-start) | collective-permute-done | bytes 131104 | tf_op jit(solution)/shard_map/while/body/eval_jaxpr/ppermute | solution.py:15
  388.6 8.2 collective-permute-done
  403.8 7.2 collective-permute-done
  417.9 9.2 collective-permute-done
  434.0 9.3 collective-permute-done
  450.3 11.8 collective-permute-done
  469.1 7.0 collective-permute-done
  483.0 6.6 collective-permute-done
  496.6 8.6 collective-permute-done
  512.1 8.5 collective-permute-done
  527.6 8.5 collective-permute-done
  543.0 8.5 collective-permute-done
  558.5 326.6 %collective-permute-done = bf16[32,2048]{1,0:T(8,128)(2,1)S(1)} collective-permute-done((bf16[32,2048]{1,0:T(8,128)(2,1)S(1)}, bf16[32,2048]{1,0:T(8,128)(2,1)S(1)}, u32[]{:S(2)}, u32[]{:S(2)}) %collective-permute-start) | collective-permute-done | bytes 131104 | tf_op jit(solution)/shard_map/while/body/eval_jaxpr/ppermute | solution.py:15
  886.0 13.0 %conditional.3 = (bf16[32,2048]{1,0:T(8,128)(2,1)S(1)}, f32[2048,128]{1,0:T(8,128)S(1)}, f32[2048,128]{1,0:T(8,128)S(1)}) conditional(s32[]{:T(128)} %convert_element_type.82, bf16[32,2048]{1,0:T(8,128)(2,1)S(1)} %dynamic-slice_select_fusion.2, (bf16[32,2048]{1,0:T(8,128)(2,1)S(1)}, s32[]{:T(128)}, f32[256,1]{0,1:T(1,128)S(1)}, ...), branch_computations={%region_2.2_spmd, %region_3.4_spmd} | conditional | flops 337711104 | bytes 14975954 | solution.py:174
  904.8 10.6 collective-permute-done
  916.3 13.0 %conditional.3 = (bf16[32,2048]{1,0:T(8,128)(2,1)S(1)}, f32[2048,128]{1,0:T(8,128)S(1)}, f32[2048,128]{1,0:T(8,128)S(1)}) conditional(s32[]{:T(128)} %convert_element_type.82, bf16[32,2048]{1,0:T(8,128)(2,1)S(1)} %dynamic-slice_select_fusion.2, (bf16[32,2048]{1,0:T(8,128)(2,1)S(1)}, s32[]{:T(128)}, f32[256,1]{0,1:T(1,128)S(1)}, ...), branch_computations={%region_2.2_spmd, %region_3.4_spmd} | conditional | flops 337711104 | bytes 14975954 | solution.py:174
  935.2 9.6 collective-permute-done
  945.7 13.0 %conditional.3 = (bf16[32,2048]{1,0:T(8,128)(2,1)S(1)}, f32[2048,128]{1,0:T(8,128)S(1)}, f32[2048,128]{1,0:T(8,128)S(1)}) conditional(s32[]{:T(128)} %convert_element_type.82, bf16[32,2048]{1,0:T(8,128)(2,1)S(1)} %dynamic-slice_select_fusion.2, (bf16[32,2048]{1,0:T(8,128)(2,1)S(1)}, s32[]{:T(128)}, f32[256,1]{0,1:T(1,128)S(1)}, ...), branch_computations={%region_2.2_spmd, %region_3.4_spmd} | conditional | flops 337711104 | bytes 14975954 | solution.py:174
  971.6 13.0 %conditional.3 = (bf16[32,2048]{1,0:T(8,128)(2,1)S(1)}, f32[2048,128]{1,0:T(8,128)S(1)}, f32[2048,128]{1,0:T(8,128)S(1)}) conditional(s32[]{:T(128)} %convert_element_type.82, bf16[32,2048]{1,0:T(8,128)(2,1)S(1)} %dynamic-slice_select_fusion.2, (bf16[32,2048]{1,0:T(8,128)(2,1)S(1)}, s32[]{:T(128)}, f32[256,1]{0,1:T(1,128)S(1)}, ...), branch_computations={%region_2.2_spmd, %region_3.4_spmd} | conditional | flops 337711104 | bytes 14975954 | solution.py:174
  990.4 6.5 collective-permute-done
  997.9 13.0 %conditional.3 = (bf16[32,2048]{1,0:T(8,128)(2,1)S(1)}, f32[2048,128]{1,0:T(8,128)S(1)}, f32[2048,128]{1,0:T(8,128)S(1)}) conditional(s32[]{:T(128)} %convert_element_type.82, bf16[32,2048]{1,0:T(8,128)(2,1)S(1)} %dynamic-slice_select_fusion.2, (bf16[32,2048]{1,0:T(8,128)(2,1)S(1)}, s32[]{:T(128)}, f32[256,1]{0,1:T(1,128)S(1)}, ...), branch_computations={%region_2.2_spmd, %region_3.4_spmd} | conditional | flops 337711104 | bytes 14975954 | solution.py:174
  1016.7 7.8 collective-permute-done
  1025.5 13.0 %conditional.3 = (bf16[32,2048]{1,0:T(8,128)(2,1)S(1)}, f32[2048,128]{1,0:T(8,128)S(1)}, f32[2048,128]{1,0:T(8,128)S(1)}) conditional(s32[]{:T(128)} %convert_element_type.82, bf16[32,2048]{1,0:T(8,128)(2,1)S(1)} %dynamic-slice_select_fusion.2, (bf16[32,2048]{1,0:T(8,128)(2,1)S(1)}, s32[]{:T(128)}, f32[256,1]{0,1:T(1,128)S(1)}, ...), branch_computations={%region_2.2_spmd, %region_3.4_spmd} | conditional | flops 337711104 | bytes 14975954 | solution.py:174
  1051.0 13.0 %conditional.3 = (bf16[32,2048]{1,0:T(8,128)(2,1)S(1)}, f32[2048,128]{1,0:T(8,128)S(1)}, f32[2048,128]{1,0:T(8,128)S(1)}) conditional(s32[]{:T(128)} %convert_element_type.82, bf16[32,2048]{1,0:T(8,128)(2,1)S(1)} %dynamic-slice_select_fusion.2, (bf16[32,2048]{1,0:T(8,128)(2,1)S(1)}, s32[]{:T(128)}, f32[256,1]{0,1:T(1,128)S(1)}, ...), branch_computations={%region_2.2_spmd, %region_3.4_spmd} | conditional | flops 337711104 | bytes 14975954 | solution.py:174
  1069.8 7.1 collective-permute-done
  1077.9 12.9 %conditional.3 = (bf16[32,2048]{1,0:T(8,128)(2,1)S(1)}, f32[2048,128]{1,0:T(8,128)S(1)}, f32[2048,128]{1,0:T(8,128)S(1)}) conditional(s32[]{:T(128)} %convert_element_type.82, bf16[32,2048]{1,0:T(8,128)(2,1)S(1)} %dynamic-slice_select_fusion.2, (bf16[32,2048]{1,0:T(8,128)(2,1)S(1)}, s32[]{:T(128)}, f32[256,1]{0,1:T(1,128)S(1)}, ...), branch_computations={%region_2.2_spmd, %region_3.4_spmd} | conditional | flops 337711104 | bytes 14975954 | solution.py:174
  1098.3 75.0 %reduce-scatter.5.cloned.1.call-done = bf16[128,128]{1,0:T(8,128)(2,1)} async-done(((bf16[2048,128]{1,0:T(8,128)(2,1)}), bf16[128,128]{1,0:T(8,128)(2,1)}) %reduce-scatter.5.cloned.1.call-update) | async-done | bytes 32784 | tf_op jit(solution)/shard_map/reduce_scatter | solution.py:191
  1174.7 65.7 %reduce-scatter.3.cloned.1.call-done = bf16[128,128]{1,0:T(8,128)(2,1)} async-done(((bf16[2048,128]{1,0:T(8,128)(2,1)}), bf16[128,128]{1,0:T(8,128)(2,1)}) %reduce-scatter.3.cloned.1.call-update) | async-done | bytes 32784 | tf_op jit(solution)/shard_map/reduce_scatter | solution.py:188
  (369 shorter events, 429.6 us)
Async XLA Ops:
  7.2 3.1 copy-start
  7.2 3.3 copy-start.6
  7.2 3.6 copy-start.7
  7.2 29.4 %copy-start.8 = (bf16[1,128,128]{2,1,0:T(8,128)(2,1)S(1)}, bf16[1,128,128]{2,1,0:T(8,128)(2,1)}, u32[]{:S(2)}) copy-start(bf16[1,128,128]{2,1,0:T(8,128)(2,1)} %param.16) | copy-start | bytes 98308
  7.2 68.6 %all-gather.5.cloned.1.call-start = ((), (), s32[]{:S(2)}) async-start(), calls=%async_computation.4 | async-start | bytes 8912896 | tf_op jit(solution)/shard_map/all_gather | solution.py:101
  7.9 1165.4 %reduce-scatter.5.cloned.1.call-start = ((), (), s32[]{:S(2)}) async-start(), calls=%async_computation.3 | async-start | bytes 557056 | tf_op jit(solution)/shard_map/reduce_scatter | solution.py:191
  61.0 3.6 copy-start.1
  75.8 7.8 copy-start.2
  87.8 11.3 collective-permute-start
  103.5 9.7 collective-permute-start
  118.9 9.2 collective-permute-start
  133.7 7.5 collective-permute-start
  146.9 12.0 collective-permute-start
  164.5 11.3 collective-permute-start
  181.5 7.6 collective-permute-start
  194.7 6.7 collective-permute-start
  207.1 9.7 collective-permute-start
  222.5 6.6 collective-permute-start
  234.7 8.4 collective-permute-start
  248.8 12.4 collective-permute-start
  266.9 9.9 collective-permute-start
  282.5 6.7 collective-permute-start
  294.8 7.9 collective-permute-start
  308.4 8.7 collective-permute-start
  322.8 7.0 collective-permute-start
  335.4 8.8 collective-permute-start
  349.8 10.2 collective-permute-start
  365.6 16.0 %collective-permute-start = (bf16[32,2048]{1,0:T(8,128)(2,1)S(1)}, bf16[32,2048]{1,0:T(8,128)(2,1)S(1)}, u32[]{:S(2)}, u32[]{:S(2)}) collective-permute-start(bf16[32,2048]{1,0:T(8,128)(2,1)S(1)} %get-tuple-element.710), channel_id=1, source_target_pairs={{16,0},{32,16},{48,32},{64,48},{80,64},{96,80},{112,96},{128,112},... | collective-permute-start | bytes 393224 | tf_op jit(solution)/shard_map/while/body/eval_jaxpr/ppermute | solution.py:15
  387.3 9.5 collective-permute-start
  402.4 8.5 collective-permute-start
  416.6 10.5 collective-permute-start
  432.7 10.6 collective-permute-start
  449.0 13.2 %collective-permute-start = (bf16[32,2048]{1,0:T(8,128)(2,1)S(1)}, bf16[32,2048]{1,0:T(8,128)(2,1)S(1)}, u32[]{:S(2)}, u32[]{:S(2)}) collective-permute-start(bf16[32,2048]{1,0:T(8,128)(2,1)S(1)} %get-tuple-element.710), channel_id=1, source_target_pairs={{16,0},{32,16},{48,32},{64,48},{80,64},{96,80},{112,96},{128,112},... | collective-permute-start | bytes 393224 | tf_op jit(solution)/shard_map/while/body/eval_jaxpr/ppermute | solution.py:15
  467.8 8.3 collective-permute-start
  481.7 7.9 collective-permute-start
  495.3 9.9 collective-permute-start
  510.8 9.8 collective-permute-start
  526.3 9.8 collective-permute-start
  541.7 9.8 collective-permute-start
  557.2 327.9 %collective-permute-start = (bf16[32,2048]{1,0:T(8,128)(2,1)S(1)}, bf16[32,2048]{1,0:T(8,128)(2,1)S(1)}, u32[]{:S(2)}, u32[]{:S(2)}) collective-permute-start(bf16[32,2048]{1,0:T(8,128)(2,1)S(1)} %get-tuple-element.710), channel_id=1, source_target_pairs={{16,0},{32,16},{48,32},{64,48},{80,64},{96,80},{112,96},{128,112},... | collective-permute-start | bytes 393224 | tf_op jit(solution)/shard_map/while/body/eval_jaxpr/ppermute | solution.py:15
  903.5 11.9 collective-permute-start
  933.8 10.9 collective-permute-start
  963.2 7.5 collective-permute-start
  989.1 7.9 collective-permute-start
  1015.4 9.1 collective-permute-start
  1043.0 7.1 collective-permute-start
  1068.5 8.4 collective-permute-start
  1097.4 143.1 %reduce-scatter.3.cloned.1.call-start = ((), (), s32[]{:S(2)}) async-start(), calls=%async_computation.2 | async-start | bytes 557056 | tf_op jit(solution)/shard_map/reduce_scatter | solution.py:188
  (3 other events, 5.9 us)
Sparse Core Ops, SparseCore 0:
  10.2 65.6 all-gather.4
  1097.5 75.7 reduce-scatter.4
  1176.3 64.0 reduce-scatter.2
where the time goes:
time: 1260 us; the launch traced here: 1250 us
  waiting for transfers between devices  786 us (62%)
  other arithmetic  244 us (19%)
  matrix products  93.4 us (7%)
  starting transfers between devices  50.1 us (4%)
  blocking collectives  49.5 us (4%)
  between operations  13.9 us (1%)
    ppermute x39, waiting for transfers between devices, shifted(): lax.ppermute(value, axis, [(source, source + steps) for source in range(f...  635 us
    add x39, other arithmetic, turn_accumulate(): return (grad_input, grads, down_sum + down_part, up_sum + up_part)  113 us
    reduce_scatter x1, waiting for transfers between devices, per_device(): lax.psum_scatter(up_total.astype(jnp.bfloat16), 'dp', scatter_dimension=0...  75 us
    reduce_scatter x1, waiting for transfers between devices, per_device(): lax.psum_scatter(down_total.astype(jnp.bfloat16), 'dp', scatter_dimension...  65.7 us
    dynamic_update_slice x39, other arithmetic, store(): return lax.dynamic_update_slice_in_dim(buffer, kept, row_start, 0)  62.4 us
    ppermute x39, starting transfers between devices, shifted(): lax.ppermute(value, axis, [(source, source + steps) for source in range(f...  49.9 us
    dot_general x8, matrix products, backward_pass(): lax.dot_general(grad_pre, weight, (((1,), (1,)), ((), ())), preferred_ele...  47.7 us
    select_n x39, other arithmetic, upstream_for(): return jnp.where(is_last, rows_of(seed_grad, row_start), incoming)  36.6 us
  transfers between devices with their start and end apart: 42, of which 42 were waited for; matrix products, arithmetic and copies ran while one was open for 1% of the time, Pallas kernels for 0%

commit v1 on v0

v1 whole, which is shorter than its diff:
```python
import functools
import math

import jax
import jax.numpy as jnp
from jax import lax
from jax.experimental import pallas as pl
from jax.experimental.pallas import tpu as pltpu
from jax.sharding import Mesh, PartitionSpec as P

EPSILON = 1e-06
AXES = ("y", "zh", "zl", "x", "c")
SIZES = (8, 4, 2, 4, 2)
STAGES, BLOCKS = SIZES[0], SIZES[1]
GROUP = ("zl", "x", "c")
PLANE = ("zh", "zl", "x", "c")
MEMBERS = 16
ROWS = 32
CHUNK = 512
SLOTS = 4
LAST_DIMS = (((1,), (1,)), ((), ()))
FIRST_DIMS = (((0,), (0,)), ((), ()))
SLOPE = math.sqrt(2.0 / math.pi)
CUBIC = 0.044715
MIB = 2**20


def dot(left, right, dims=(((1,), (0,)), ((), ()))):
    return lax.dot_general(left, right, dims, preferred_element_type=jnp.float32)


def per_batch_modulation(from_table, to_table, level_pairs):
    ladder = jnp.arange(from_table.shape[0], dtype=jnp.int32)[None, :]
    hot_from = (level_pairs[:, 0:1] == ladder).astype(jnp.bfloat16)
    hot_to = (level_pairs[:, 1:2] == ladder).astype(jnp.bfloat16)
    return dot(hot_from, from_table) + dot(hot_to, to_table)


def forward_kernel(batches, width, place, x, mod, target, wd, up, own_down, own_up, d, h, inv, *rest):
    seeds, (downs, columns, sems, own_sems) = rest[:batches], rest[batches:]
    chunks = width // CHUNK
    total = BLOCKS * chunks
    own = (
        pltpu.make_async_copy(wd.at[place[0], :, width:], own_down, own_sems.at[0]),
        pltpu.make_async_copy(up.at[place[0]], own_up, own_sems.at[1]),
    )

    def fetch_down(b):
        return pltpu.make_async_copy(wd.at[b, :, width:], downs.at[b], sems.at[0, b])

    def fetch_columns(index):
        b, j, slot = BLOCKS - 1 - index // chunks, index % chunks, index % SLOTS
        return pltpu.make_async_copy(wd.at[b, :, pl.ds(j * CHUNK, CHUNK)], columns.at[slot], sems.at[1, slot])

    for index in range(total):
        b, j = BLOCKS - 1 - index // chunks, index % chunks
        if index == 0:
            fetch_down(b).start()
            for ahead in range(SLOTS):
                fetch_columns(ahead).start()
            for other in reversed(range(BLOCKS - 1)):
                fetch_down(other).start()
            for copy in own:
                copy.start()
        if j == 0:
            pieces = []
            for m in range(batches):
                r = pl.ds(m * ROWS, ROWS)
                values = x[b, r, :].astype(jnp.float32)
                rms = lax.rsqrt(jnp.mean(values * values, axis=1, keepdims=True) + EPSILON)
                normed = values * rms
                h[b, r, :] = normed
                inv[b, r, :] = jnp.broadcast_to(rms, (ROWS, inv.shape[2]))
                shift = mod[b, pl.ds(m, 1), 0:width]
                scale = mod[b, pl.ds(m, 1), width : 2 * width]
                pieces.append((normed * (1.0 + scale) + shift).astype(jnp.bfloat16))
            modulated = jnp.concatenate(pieces, axis=0)
            fetch_down(b).wait()
            low = dot(modulated, downs[b]).astype(jnp.bfloat16)
        c = pl.ds(j * CHUNK, CHUNK)
        fetch_columns(index).wait()
        pre = dot(modulated, columns[index % SLOTS]) + dot(low, up[b, c, :], LAST_DIMS)
        if index + SLOTS < total:
            fetch_columns(index + SLOTS).start()
        squared = pre * pre
        bent = jnp.tanh(SLOPE * pre * (1.0 + CUBIC * squared))
        half = 0.5 * (1.0 + bent)
        slope = half + 0.5 * pre * (1.0 - bent * bent) * (SLOPE * (1.0 + 3.0 * CUBIC * squared))
        for m in range(batches):
            s = slice(m * ROWS, (m + 1) * ROWS)
            gate = mod[b, pl.ds(m, 1), pl.ds(2 * width + j * CHUNK, CHUNK)]
            d[b, s, c] = slope[s] * gate
            if b == BLOCKS - 1:
                out = x[b, s, c].astype(jnp.float32) + gate * (pre[s] * half[s])
                seeds[m][:, c] = (out - target[s, c].astype(jnp.float32)).astype(jnp.bfloat16)
    for copy in own:
        copy.wait()


def chain_kernel(active_stage, m, width, stage, gin, wd, up, d, h, mod, inv, gs_in, us_in, gout, gs, us, g_keep, u_keep, sems):
    r = pl.ds(m * ROWS, ROWS)

    def store_u(b):
        return pltpu.make_async_copy(u_keep.at[b], us.at[b, r, :], sems.at[0, b])

    def store_g(b):
        return pltpu.make_async_copy(g_keep.at[b], gs.at[b, r, :], sems.at[1, b])

    def block(step, carry):
        b = BLOCKS - 1 - step
        u = (d[b, r, :] * gout[...].astype(jnp.float32)).astype(jnp.bfloat16)
        u_keep[b] = u
        store_u(b).start()
        low = dot(u, up[b]).astype(jnp.bfloat16)
        scaled, total = [], None
        for j in range(width // CHUNK):
            c = pl.ds(j * CHUNK, CHUNK)
            grad = dot(u, wd[b, c, :width], LAST_DIMS) + dot(low, wd[b, c, width:], LAST_DIMS)
            grad = grad * (1.0 + mod[b, pl.ds(m, 1), pl.ds(width + j * CHUNK, CHUNK)])
            scaled.append(grad)
            part = jnp.sum(grad * h[b, r, c], axis=1, keepdims=True)
            total = part if total is None else total + part
        centred = total * (1.0 / width)
        rms = inv[b, r, 0:1]
        for j in range(width // CHUNK):
            c = pl.ds(j * CHUNK, CHUNK)
            upstream = gout[:, c].astype(jnp.float32)
            value = (upstream + rms * (scaled[j] - h[b, r, c] * centred)).astype(jnp.bfloat16)
            gout[:, c] = value
            g_keep[b, :, c] = value
        store_g(b).start()
        return carry

    @pl.when(stage[0] == active_stage)
    def run():
        gout[...] = gin[...]
        lax.fori_loop(0, BLOCKS, block, 0)
        for b in range(BLOCKS):
            store_u(b).wait()
            store_g(b).wait()


VMEM = pl.BlockSpec(memory_space=pltpu.VMEM)
ANY = pl.BlockSpec(memory_space=pl.ANY)
SMEM = pl.BlockSpec(memory_space=pltpu.SMEM)


def resident(value):
    return pltpu.with_memory_space_constraint(value, pltpu.VMEM)


def per_device(block_inputs, target, frozen_weight, adapter_down, adapter_up, start_modulation, finish_modulation, level_pairs):
    stage = lax.axis_index("y")
    place = lax.axis_index("zh")
    tokens, width = block_inputs.shape[1:]
    rank = adapter_down.shape[2]
    share = tokens // BLOCKS
    batches = share // ROWS
    grad_scale = 1.0 / math.sqrt(tokens * MEMBERS)

    wd = jnp.concatenate([frozen_weight[0], adapter_down[0]], axis=1)
    wd = lax.all_gather(wd, PLANE, axis=0, tiled=True).reshape(BLOCKS, width, width + rank)
    up = lax.all_gather(adapter_up[0], PLANE, axis=0, tiled=True).reshape(BLOCKS, width, rank)

    own_mod = per_batch_modulation(start_modulation[0], finish_modulation[0], level_pairs)
    mod = lax.all_to_all(own_mod, "zh", 0, 0, tiled=True).reshape(BLOCKS, batches, 3 * width)
    x = lax.all_to_all(block_inputs[0], "zh", 0, 0, tiled=True).reshape(BLOCKS, share, width)

    own_target = lax.dynamic_slice_in_dim(target, place * share, share, 0)
    stage = stage.astype(jnp.int32).reshape(1)
    place = place.astype(jnp.int32).reshape(1)
    values = block_inputs[0].astype(jnp.float32)
    normed = values * lax.rsqrt(jnp.mean(values * values, axis=1, keepdims=True) + EPSILON)
    row_mod = jnp.repeat(own_mod[:, : 2 * width], ROWS, axis=0)
    modulated = (normed * (1.0 + row_mod[:, width:]) + row_mod[:, :width]).astype(jnp.bfloat16)
    gs = jnp.zeros((BLOCKS, share, width), jnp.bfloat16)
    us = jnp.zeros((BLOCKS, share, width), jnp.bfloat16)
    x, mod, stage, place, own_target, modulated, gs, us = lax.optimization_barrier(
        (x, mod, stage, place, own_target, modulated, gs, us)
    )
    wd_near, up_near, mod_near = resident(wd), resident(up), resident(mod)
    own_down, own_up, d, h, inv, *arrived = pl.pallas_call(
        functools.partial(forward_kernel, batches, width),
        out_shape=[
            jax.ShapeDtypeStruct((width, rank), wd.dtype),
            jax.ShapeDtypeStruct((width, rank), up.dtype),
            pltpu.VMEM((BLOCKS, share, width), jnp.float32),
            pltpu.VMEM((BLOCKS, share, width), jnp.float32),
            pltpu.VMEM((BLOCKS, share, rank), jnp.float32),
        ]
        + [pltpu.VMEM((ROWS, width), jnp.bfloat16)] * batches,
        in_specs=[SMEM] + [VMEM] * 3 + [ANY, VMEM],
        out_specs=[ANY] * 2 + [VMEM] * (3 + batches),
        scratch_shapes=[
            pltpu.VMEM((BLOCKS, width, rank), jnp.bfloat16),
            pltpu.VMEM((SLOTS, width, CHUNK), jnp.bfloat16),
            pltpu.SemaphoreType.DMA((2, BLOCKS)),
            pltpu.SemaphoreType.DMA((2,)),
        ],
        compiler_params=pltpu.CompilerParams(vmem_limit_bytes=16 * MIB),
        name="forward",
    )(place, x, mod_near, own_target, wd, up_near)

    d_near, h_near, inv_near = (resident(v) for v in (d, h, inv))
    for step in range(STAGES):
        for m in range(batches):
            gout, gs, us = pl.pallas_call(
                functools.partial(chain_kernel, STAGES - 1 - step, m, width),
                out_shape=[
                    jax.ShapeDtypeStruct((ROWS, width), jnp.bfloat16),
                    jax.ShapeDtypeStruct(gs.shape, gs.dtype),
                    jax.ShapeDtypeStruct(us.shape, us.dtype),
                ],
                in_specs=[SMEM] + [VMEM] * 7 + [ANY] * 2,
                out_specs=[VMEM, ANY, ANY],
                scratch_shapes=[
                    pltpu.VMEM((BLOCKS, ROWS, width), jnp.bfloat16),
                    pltpu.VMEM((BLOCKS, ROWS, width), jnp.bfloat16),
                    pltpu.SemaphoreType.DMA((2, BLOCKS)),
                ],
                input_output_aliases={8: 1, 9: 2},
                compiler_params=pltpu.CompilerParams(vmem_limit_bytes=8 * MIB),
                cost_estimate=pl.CostEstimate(flops=2 * BLOCKS * ROWS * width * width, bytes_accessed=4 * MIB, transcendentals=0),
                name="relay",
            )(stage, resident(arrived[m]), wd_near, up_near, d_near, h_near, mod_near, inv_near, gs, us)
            if step < STAGES - 1:
                arrived[m] = lax.ppermute(gout, "y", [(STAGES - 1 - step, STAGES - 2 - step)])

    gs, us, modulated, own_down, own_up = lax.optimization_barrier((gs, us, modulated, own_down, own_up))
    grads = lax.all_to_all(gs.reshape(tokens, width), "zh", 0, 0, tiled=True)
    own_pre = lax.all_to_all(us.reshape(tokens, width), "zh", 0, 0, tiled=True)

    lowrank = dot(modulated, own_down).astype(jnp.bfloat16)
    grad_low = dot(own_pre, own_up).astype(jnp.bfloat16)
    down_part = dot(modulated, grad_low, FIRST_DIMS).astype(jnp.bfloat16)
    up_part = dot(own_pre, lowrank, FIRST_DIMS).astype(jnp.bfloat16)
    owned = width // MEMBERS
    parts = jnp.concatenate([down_part.reshape(MEMBERS, owned, rank), up_part.reshape(MEMBERS, owned, rank)], axis=1)
    parts = lax.all_to_all(parts, GROUP, 0, 0, tiled=True)
    total = jnp.sum(parts.astype(jnp.float32), axis=0) * grad_scale
    return grads[None], total[None, :owned], total[None, owned:]


def solution(mesh):
    split = Mesh(mesh.devices.reshape(SIZES), AXES)
    blocks = ("y", "zh")
    return jax.shard_map(
        per_device,
        mesh=split,
        in_specs=(
            P(blocks, GROUP, None),
            P(GROUP, None),
            P(blocks, GROUP, None),
            P(blocks, GROUP, None),
            P(blocks, GROUP, None),
            P(blocks, None, None),
            P(blocks, None, None),
            P(GROUP, None),
        ),
        out_specs=(P(blocks, GROUP, None), P(blocks, GROUP, None), P(blocks, GROUP, None)),
        check_vma=False,
    )
```

time: 1260 us -> 539 us (0.43)
  waiting for transfers between devices: 786 us -> 365 us
  other arithmetic: 244 us -> 7.56 us
  matrix products: 93.4 us -> 5.49 us
  Pallas kernels: 0 us -> 43.3 us
    ppermute x39 -> x14, waiting for transfers between devices: 635 us -> 118 us  [per_device(): lax.ppermute(gout, 'y', [(STAGES - 1 - step, STAGES - 2 - step)])]
    all_gather x1 -> x2, waiting for transfers between devices: 9.44 us -> 206 us  [the longest x1 155 us: per_device(): lax.all_gather(wd, PLANE, axis=0, tiled=True)]
    reduce_scatter x2 -> x0, waiting for transfers between devices: 141 us -> none  [the longest x1 75 us: per_device(): lax.psum_scatter(up_total.astype(jnp.bfloat16), 'dp', scatter_dimension=0...]
    add x39 -> x0, other arithmetic: 113 us -> none  [turn_accumulate(): return (grad_input, grads, down_sum + down_part, up_sum + up_part)]
    dot_general x45 -> x4, matrix products: 93.4 us -> 5.49 us  [dot(): lax.dot_general(left, right, dims, preferred_element_type=jnp.float32)]
    dynamic_update_slice x39 -> x0, other arithmetic: 62.4 us -> none  [store(): return lax.dynamic_update_slice_in_dim(buffer, kept, row_start, 0)]
    all_gather x2 -> x0, blocking collectives: 49.5 us -> none  [the longest x1 25.8 us: per_device(): lax.all_gather(adapter_down_weight[0], 'dp', axis=0, tiled=True)]
    pallas_call x0 -> x17, Pallas kernels: none -> 43.3 us  [the longest x16 30 us: per_device(): pl.pallas_call(functools.partial(chain_kernel, STAGES - 1 - step, m, widt...]
  transfers between devices with their start and end apart: 42 -> 19, of which waited for: 42 -> 7; matrix products, arithmetic and copies ran while one was open for 1% -> 3% of each run, Pallas kernels for 0% -> 3%
where the time goes in v1:
time: 539 us; the launch traced here: 538 us
  waiting for transfers between devices  365 us (68%)
  starting transfers between devices  43.4 us (8%)
  Pallas kernels  43.3 us (8%)
  blocking collectives  38.8 us (7%)
  local copies, waits for them, and re-layouts  19.6 us (4%)
  between operations  14.5 us (3%)
  other arithmetic  7.56 us (1%)
  matrix products  5.49 us (1%)
    all_gather x1, waiting for transfers between devices, per_device(): lax.all_gather(wd, PLANE, axis=0, tiled=True)  155 us
    ppermute x14, waiting for transfers between devices, per_device(): lax.ppermute(gout, 'y', [(STAGES - 1 - step, STAGES - 2 - step)])  118 us
    all_gather x1, waiting for transfers between devices, per_device(): lax.all_gather(adapter_up[0], PLANE, axis=0, tiled=True)  51.8 us
    pallas_call x16, Pallas kernels, per_device(): pl.pallas_call(functools.partial(chain_kernel, STAGES - 1 - step, m, widt...  30 us
    all_to_all x1, starting transfers between devices, per_device(): parts = lax.all_to_all(parts, GROUP, 0, 0, tiled=True)  24.4 us
    all_to_all x1, blocking collectives, per_device(): own_pre = lax.all_to_all(us.reshape(tokens, width), 'zh', 0, 0, tiled=True)  20.2 us
    all_to_all x1, blocking collectives, per_device(): lax.all_to_all(own_mod, 'zh', 0, 0, tiled=True)  18.6 us
    unnamed x20, local copies, waits for them, and re-layouts  16.5 us
  transfers between devices with their start and end apart: 19, of which 7 were waited for; matrix products, arithmetic and copies ran while one was open for 3% of the time, Pallas kernels for 3%

profile of v1, /device:TPU:1, one launch (start us, length us, event | category | flops | bytes accessed | tf_op | source)
XLA Modules:
  0.0 538.2 jit_solution(17365303857243546158)
XLA Ops:
  7.2 0.7 all-gather.6.cloned.1.call-update
  8.0 1.9 pad_maximum_fusion.1
  9.9 0.8 slice_bitcast_fusion.2
  10.7 1.1 fusion.5
  11.8 0.2 convolution_add_fusion
  12.2 18.6 %all_to_all.38.mod = f32[4,2,6144]{2,1,0:T(2,128)S(1)} all-to-all(f32[4,2,6144]{2,1,0:T(2,128)S(1)} %all_to_all.27), channel_id=1, replica_groups=mesh['y'=8,'zh'=4,'zl'=2,'x'=4,'c'=2] {'zh'}, dimensions={0} | all-to-all | bytes 393216 | tf_op jit(solution)/shard_map/all_to_all | solution.py:166
  30.8 3.9 all-to-all-start
  34.7 1.5 fusion
  36.3 0.5 broadcast_in_dim.14
  36.8 2.9 fusion.3
  39.7 12.8 %all-to-all-done.x = bf16[4,64,2048]{2,1,0:T(8,128)(2,1)S(1)} async-done(((bf16[4,64,2048]{2,1,0:T(8,128)(2,1)}), bf16[4,64,2048]{2,1,0:T(8,128)(2,1)S(1)}, u32[]{:S(2)}, u32[]{:S(2)}) %all-to-all-start) | async-done | bytes 1048608 | tf_op jit(solution)/shard_map/all_to_all | solution.py:167
  52.5 1.1 broadcast.14.gs_in
  53.6 1.2 copy.44.us_in
  54.8 51.8 %all-gather.6.cloned.1.call-done = bf16[1,8192,128]{2,1,0:T(8,128)(2,1)} async-done(((bf16[1,128,128]{2,1,0:T(8,128)(2,1)}), bf16[1,8192,128]{2,1,0:T(8,128)(2,1)}) %all-gather.6.cloned.1.call-update) | async-done | bytes 2097168 | tf_op jit(solution)/shard_map/all_gather | solution.py:163
  106.6 154.6 %all-gather.4.cloned.1.call-done = bf16[8192,2176]{1,0:T(8,128)(2,1)} async-done(((bf16[128,2176]{1,0:T(8,128)(2,1)}), bf16[8192,2176]{1,0:T(8,128)(2,1)}) %all-gather.4.cloned.1.call-update) | async-done | bytes 35651600 | tf_op jit(solution)/shard_map/all_gather | solution.py:162
  261.2 1.6 copy-done.3
  262.8 13.3 %forward.1 = (bf16[2048,128]{1,0:T(8,128)(2,1)S(1)}, bf16[2048,128]{1,0:T(8,128)(2,1)S(1)}, f32[4,64,2048]{2,1,0:T(8,128)S(1)}, f32[4,64,2048]{2,1,0:T(8,128)S(1...) custom-call(s32[1]{0:T(128)} %bitcast.6.place, ...), custom_call_target="tpu_custom_call" | custom-call | tf_op jit(solution)/shard_map/forward/pallas_call | solution.py:182
  276.1 11.3 %copy-done.2 = bf16[8192,2176]{1,0:T(8,128)(2,1)S(1)} copy-done((bf16[8192,2176]{1,0:T(8,128)(2,1)S(1)}, bf16[8192,2176]{1,0:T(8,128)(2,1)}, u32[]{:S(2)}) %copy-start.2) | copy-done | bytes 35651608
  287.5 0.7 collective-permute-start.1
  288.2 0.3 relay.17
  288.5 0.7 collective-permute-start
  289.3 0.7 collective-permute-start.3
  290.1 0.7 collective-permute-start.2
  290.8 0.7 collective-permute-start.5
  291.6 0.7 collective-permute-start.4
  292.4 0.7 collective-permute-start.7
  293.2 0.7 collective-permute-start.6
  294.0 0.7 collective-permute-start.9
  294.6 0.3 relay.25
  294.9 0.7 collective-permute-start.8
  295.7 0.7 collective-permute-start.11
  296.5 0.7 collective-permute-start.10
  297.3 1.3 collective-permute-start.13
  298.7 1.3 collective-permute-start.12
  300.0 117.3 %collective-permute-done.13.gin = bf16[32,2048]{1,0:T(8,128)(2,1)S(1)} collective-permute-done((bf16[32,2048]{1,0:T(8,128)(2,1)S(1)}, bf16[32,2048]{1,0:T(8,128)(2,1)S(1)}, u32[]{:S(2)}, u32[]{:S(2)}) %collective-permute-start.13) | collective-permute-done | bytes 131104 | tf_op jit(solution)/shard_map/ppermute | solution.py:227
  417.3 14.2 %relay.30 = (bf16[32,2048]{1,0:T(8,128)(2,1)}, bf16[4,64,2048]{2,1,0:T(8,128)(2,1)}, bf16[4,64,2048]{2,1,0:T(8,128)(2,1)S(1)}) custom-call(s32[1]{0:T(128)} %bitcast.5.stage, bf16[32,2048]{1,0:T(8,128)(2,1)S(1)} %collective-permute-done.13.gin, bf16[4,2048,2176]{2,1,0:T(8,128)(2,1)S(1)} %bitcast.51, ...), custom_call_target="tpu_custom_call", output_to_operand_aliasing={{1}: (8, {}), {2}: (9, {})} | custom-call | flops 1073741824 | bytes 4194304 | tf_op jit(solution)/shard_map/relay/pallas_call | solution.py:207
  431.5 0.9 collective-permute-done.12.gin
  432.4 14.2 %relay.31 = (bf16[32,2048]{1,0:T(8,128)(2,1)}, bf16[4,64,2048]{2,1,0:T(8,128)(2,1)}, bf16[4,64,2048]{2,1,0:T(8,128)(2,1)S(1)}) custom-call(s32[1]{0:T(128)} %bitcast.5.stage, bf16[32,2048]{1,0:T(8,128)(2,1)S(1)} %collective-permute-done.12.gin, bf16[4,2048,2176]{2,1,0:T(8,128)(2,1)S(1)} %bitcast.52, ...), custom_call_target="tpu_custom_call", output_to_operand_aliasing={{1}: (8, {}), {2}: (9, {})} | custom-call | flops 1073741824 | bytes 4194304 | tf_op jit(solution)/shard_map/relay/pallas_call | solution.py:207
  446.7 20.2 %all_to_all.39 = bf16[4,64,2048]{2,1,0:T(8,128)(2,1)} all-to-all(bf16[4,64,2048]{2,1,0:T(8,128)(2,1)S(1)} %get-tuple-element.132), channel_id=1, replica_groups=mesh['y'=8,'zh'=4,'zl'=2,'x'=4,'c'=2] {'zh'}, dimensions={0} | all-to-all | bytes 2097152 | tf_op jit(solution)/shard_map/all_to_all | solution.py:231
  466.9 4.4 all-to-all-start.2
  471.3 2.1 convolution_convert_fusion
  473.4 2.1 convolution_convert_fusion.1
  475.5 1.1 pad_maximum_fusion
  476.6 11.4 %all-to-all-done.2 = bf16[4,64,2048]{2,1,0:T(8,128)(2,1)} async-done(((bf16[4,64,2048]{2,1,0:T(8,128)(2,1)}), bf16[4,64,2048]{2,1,0:T(8,128)(2,1)}, u32[]{:S(2)}, u32[]{:S(2)}) %all-to-all-start.2) | async-done | bytes 1048608 | tf_op jit(solution)/shard_map/all_to_all | solution.py:230
  488.0 24.4 %all-to-all-start.4 = ((bf16[16,256,128]{2,1,0:T(8,128)(2,1)}), bf16[16,256,128]{2,1,0:T(8,128)(2,1)S(1)}, u32[]{:S(2)}, u32[]{:S(2)}) async-start(bf16[16,256,128]{2,1,0:T(8,128)(2,1)} %pad_maximum_fusion), calls=%async_computation.4 | async-start | bytes 2097152 | tf_op jit(solution)/shard_map/all_to_all | solution.py:239
  512.4 15.8 %all-to-all-done.4 = bf16[16,256,128]{2,1,0:T(8,128)(2,1)S(1)} async-done(((bf16[16,256,128]{2,1,0:T(8,128)(2,1)}), bf16[16,256,128]{2,1,0:T(8,128)(2,1)S(1)}, u32[]{:S(2)}, u32[]{:S(2)}) %all-to-all-start.4) | async-done | bytes 1048608 | tf_op jit(solution)/shard_map/all_to_all | solution.py:239
  528.4 0.7 slice_bitcast_fusion
  529.1 2.3 copy.76
  (49 shorter events, 1.5 us)
Async XLA Ops:
  7.2 29.1 %copy-start = (bf16[256,2048]{1,0:T(8,128)(2,1)S(1)}, bf16[256,2048]{1,0:T(8,128)(2,1)}, u32[]{:S(2)}) copy-start(bf16[256,2048]{1,0:T(8,128)(2,1)} %param.9) | copy-start | bytes 3145732
  7.2 4.6 copy-start.8
  7.2 99.4 %all-gather.6.cloned.1.call-start = ((), (), s32[]{:S(2)}) async-start(), calls=%async_computation.6 | async-start | bytes 2129920 | tf_op jit(solution)/shard_map/all_gather | solution.py:163
  7.9 253.3 %all-gather.4.cloned.1.call-start = ((), (), s32[]{:S(2)}) async-start(), calls=%async_computation.5 | async-start | bytes 36208640 | tf_op jit(solution)/shard_map/all_gather | solution.py:162
  30.8 21.7 %all-to-all-start = ((bf16[4,64,2048]{2,1,0:T(8,128)(2,1)}), bf16[4,64,2048]{2,1,0:T(8,128)(2,1)S(1)}, u32[]{:S(2)}, u32[]{:S(2)}) async-start(bf16[4,64,2048]{2,1,0:T(8,128)(2,1)} %bitcast), calls=%async_computation | async-start | bytes 2097152 | tf_op jit(solution)/shard_map/all_to_all | solution.py:167
  261.2 1.6 copy-start.3
  262.8 13.3 %copy-start.4 = (bf16[1,8192,128]{2,1,0:T(8,128)(2,1)S(1)}, bf16[1,8192,128]{2,1,0:T(8,128)(2,1)}, u32[]{:S(2)}) copy-start(bf16[1,8192,128]{2,1,0:T(8,128)(2,1)} %all-gather.6.cloned.1.call-done) | copy-start | bytes 6291460
  276.1 11.4 %copy-start.5 = (bf16[2048,128]{1,0:T(8,128)(2,1)}, bf16[2048,128]{1,0:T(8,128)(2,1)S(1)}, u32[]{:S(2)}) copy-start(bf16[2048,128]{1,0:T(8,128)(2,1)S(1)} %get-tuple-element.134) | copy-start | bytes 1572868
  276.1 11.3 %copy-start.2 = (bf16[8192,2176]{1,0:T(8,128)(2,1)S(1)}, bf16[8192,2176]{1,0:T(8,128)(2,1)}, u32[]{:S(2)}) copy-start(bf16[8192,2176]{1,0:T(8,128)(2,1)} %all-gather.4.cloned.1.call-done) | copy-start | bytes 106954752
  287.5 1.6 collective-permute-start.1
  288.5 1.5 collective-permute-start
  289.3 1.5 collective-permute-start.3
  290.1 1.5 collective-permute-start.2
  290.8 1.5 collective-permute-start.5
  291.6 1.5 collective-permute-start.4
  292.4 1.5 collective-permute-start.7
  293.2 1.5 collective-permute-start.6
  294.0 1.7 collective-permute-start.9
  294.9 1.5 collective-permute-start.8
  295.7 1.5 collective-permute-start.11
  296.5 2.1 collective-permute-start.10
  297.3 120.0 %collective-permute-start.13 = (bf16[32,2048]{1,0:T(8,128)(2,1)S(1)}, bf16[32,2048]{1,0:T(8,128)(2,1)S(1)}, u32[]{:S(2)}, u32[]{:S(2)}) collective-permute-start(bf16[32,2048]{1,0:T(8,128)(2,1)S(1)} %get-tuple-element.120), channel_id=1, source_target_pairs={{64,0},{65,1},{66,2},{67,3},{68,4},{69,5},{70,6},{71,7},{72,8},{73... | collective-permute-start | bytes 393224 | tf_op jit(solution)/shard_map/ppermute | solution.py:227
  298.7 133.8 %collective-permute-start.12 = (bf16[32,2048]{1,0:T(8,128)(2,1)S(1)}, bf16[32,2048]{1,0:T(8,128)(2,1)S(1)}, u32[]{:S(2)}, u32[]{:S(2)}) collective-permute-start(bf16[32,2048]{1,0:T(8,128)(2,1)S(1)} %get-tuple-element.119), channel_id=1, source_target_pairs={{64,0},{65,1},{66,2},{67,3},{68,4},{69,5},{70,6},{71,7},{72,8},{73... | collective-permute-start | bytes 393224 | tf_op jit(solution)/shard_map/ppermute | solution.py:227
  446.7 24.6 %copy-start.6 = (bf16[2048,128]{1,0:T(8,128)(2,1)S(1)}, bf16[2048,128]{1,0:T(8,128)(2,1)}, u32[]{:S(2)}) copy-start(bf16[2048,128]{1,0:T(8,128)(2,1)} %copy-done.5) | copy-start | bytes 1572868
  466.9 4.4 copy-start.7
  466.9 21.1 %all-to-all-start.2 = ((bf16[4,64,2048]{2,1,0:T(8,128)(2,1)}), bf16[4,64,2048]{2,1,0:T(8,128)(2,1)}, u32[]{:S(2)}, u32[]{:S(2)}) async-start(bf16[4,64,2048]{2,1,0:T(8,128)(2,1)} %get-tuple-element.130), calls=%async_computation.2 | async-start | bytes 2097152 | tf_op jit(solution)/shard_map/all_to_all | solution.py:230
  488.0 40.3 %all-to-all-start.4 = ((bf16[16,256,128]{2,1,0:T(8,128)(2,1)}), bf16[16,256,128]{2,1,0:T(8,128)(2,1)S(1)}, u32[]{:S(2)}, u32[]{:S(2)}) async-start(bf16[16,256,128]{2,1,0:T(8,128)(2,1)} %pad_maximum_fusion), calls=%async_computation.4 | async-start | bytes 2097152 | tf_op jit(solution)/shard_map/all_to_all | solution.py:239
  512.4 19.0 %copy-start.1 = (bf16[256,2048]{1,0:T(8,128)(2,1)S(1)}, bf16[256,2048]{1,0:T(8,128)(2,1)}, u32[]{:S(2)}) copy-start(bf16[256,2048]{1,0:T(8,128)(2,1)} %param.9) | copy-start | bytes 3145732
Sparse Core Ops, SparseCore 0:
  11.4 95.1 all-gather.5
  109.9 151.2 all-gather.3
